TPU v7x, 32 devices: a whole 2x2x4 slice. The times are simulated.
32 devices in a mesh: groups: 2 (over x), ctx: 16 (over z, y, core).
Axes of the slice: x: 2, y: 2, z: 4, core: 2. Of those that a mesh axis runs over, the one named last changes fastest.
Arguments:
- queries: bfloat16 [64, 8192], P(('groups', 'ctx')), parts along dimension 0, may hold values from -256 to 256, as said below
- cached_key_rows: bfloat16 [16384, 1024], P(('groups', 'ctx')), parts along dimension 0, may hold values from -4 to 4, as said below
- cached_value_rows: bfloat16 [16384, 1024], P(('groups', 'ctx')), parts along dimension 0, may hold values from -6 to 6
- cache_position: int32 [16384], P(('groups', 'ctx')), parts along dimension 0, may hold values from 0 to 8191, as said below
- lengths: int32 [64], P(('groups', 'ctx')), parts along dimension 0, may hold values from 2 to 8192, as said below
- norm_gain: float32 [8192], replicated, may hold values from 0.5 to 1.5
- gate_weight: bfloat16 [14336, 8192], P('ctx'), may hold values from -0.0625 to 0.0625
- up_weight: bfloat16 [14336, 8192], P('ctx'), may hold values from -0.0625 to 0.0625
- down_weight: bfloat16 [14336, 8192], P('ctx'), may hold values from -0.046875 to 0.046875
Outputs:
- layer_out: bfloat16 [64, 8192], P(('groups', 'ctx')), parts along dimension 0
There are 2 independent parts, one for each index of `groups`. A program takes and returns all parts, laid end to end along the dimension named above; an argument that names none is the same for every part. Nothing has to cross between parts.
Inputs may be any that keep to these rules, and one draw needn't show every extreme that they name: `queries`: queries stay within the stated range. `cached_key_rows`: keys stay within the stated range. `cache_position`: A permutation of 0 to 8191. `lengths`: some row has length 8192 and some row has length 2.
All inputs are finite; a program needn't handle non-finite values.
Results may differ from a plain program's by a relative error of at most 0.02.
Values may be sent and summed in bfloat16 or wider, within the bound.
A program may use at most 128 MiB of HBM per device.

v0:
```python
import jax
import jax.numpy as jnp
from jax import lax
from jax.sharding import PartitionSpec as P

D = 8192
QUERY_HEADS = 64
KEY_VALUE_HEADS = 8
HEAD_SIZE = 128


def partial_softmax(
    query_row_matrix, row_lengths, cached_key_rows, cached_value_rows, cache_position
):
    count_of_rows = query_row_matrix.shape[0]
    count_of_slots = cached_key_rows.shape[0]
    query_group_size = QUERY_HEADS // KEY_VALUE_HEADS
    query_head_count = query_row_matrix.reshape(
        count_of_rows, KEY_VALUE_HEADS, query_group_size, HEAD_SIZE
    )
    key_head_count = cached_key_rows.reshape(count_of_slots, KEY_VALUE_HEADS, HEAD_SIZE)
    value_head_count = cached_value_rows.reshape(count_of_slots, KEY_VALUE_HEADS, HEAD_SIZE)
    scores = jnp.einsum(
        "rkgd,tkd->rkgt", query_head_count, key_head_count, preferred_element_type=jnp.float32
    ) * HEAD_SIZE ** (-0.5)
    live = (cache_position[None, :] < row_lengths[:, None])[:, None, None, :]
    scores = jnp.where(live, scores, -1e30)
    peak = jnp.max(scores, axis=3)
    weights = jnp.where(live, jnp.exp(scores - peak[..., None]), 0.0)
    totals = jnp.sum(weights, axis=3)
    summed = jnp.einsum(
        "rkgt,tkd->rkgd",
        weights.astype(jnp.bfloat16),
        value_head_count,
        preferred_element_type=jnp.float32,
    )
    return (
        peak.reshape(count_of_rows, QUERY_HEADS),
        totals.reshape(count_of_rows, QUERY_HEADS),
        summed.reshape(count_of_rows, QUERY_HEADS, HEAD_SIZE),
    )


def local(
    queries,
    cached_key_rows,
    cached_value_rows,
    cache_position,
    lengths,
    norm_gain,
    gate_weight,
    up_weight,
    down_weight,
):
    cycle_size = lax.axis_size("ctx")
    row_dev = queries.shape[0]
    all_lengths = lax.all_gather(lengths, "ctx", axis=0, tiled=True)
    every_query = lax.all_gather(queries, "ctx", axis=0, tiled=True)
    count_of_blocks = cycle_size // 8
    block_rows = row_dev * 8

    def one_block(pieces):
        return partial_softmax(
            pieces[0], pieces[1], cached_key_rows, cached_value_rows, cache_position
        )

    peak_all, totals_all, summed_all = lax.map(
        one_block,
        (
            every_query.reshape(count_of_blocks, block_rows, D),
            all_lengths.reshape(count_of_blocks, block_rows),
        ),
    )
    peak_all = peak_all.reshape(cycle_size, row_dev, QUERY_HEADS)
    totals_all = totals_all.reshape(cycle_size, row_dev, QUERY_HEADS)
    summed_all = summed_all.reshape(cycle_size, row_dev, QUERY_HEADS, HEAD_SIZE)
    peak_all, totals_all, summed_all = (
        lax.all_to_all(peak_all, "ctx", split_axis=0, concat_axis=0, tiled=True),
        lax.all_to_all(totals_all, "ctx", split_axis=0, concat_axis=0, tiled=True),
        lax.all_to_all(summed_all, "ctx", split_axis=0, concat_axis=0, tiled=True),
    )
    peak = jnp.max(peak_all, axis=0)
    scaling = jnp.exp(peak_all - peak[None])
    totals = jnp.sum(totals_all * scaling, axis=0)
    summed = jnp.sum(summed_all * scaling[..., None], axis=0)
    attended = (summed / totals[..., None]).reshape(row_dev, D).astype(jnp.bfloat16)
    widened = attended.astype(jnp.float32)
    mean_square = jnp.mean(widened * widened, axis=1, keepdims=True) + 1e-05
    normed = (widened * lax.rsqrt(mean_square) * norm_gain[None, :]).astype(jnp.bfloat16)
    piece = lax.all_gather(normed, "ctx", axis=0, tiled=True)
    gate = lax.dot_general(
        piece, gate_weight, (((1,), (1,)), ((), ())), preferred_element_type=jnp.float32
    )
    upward = lax.dot_general(
        piece, up_weight, (((1,), (1,)), ((), ())), preferred_element_type=jnp.float32
    )
    activated = (jax.nn.silu(gate) * upward).astype(jnp.bfloat16)
    layer_sum = lax.psum_scatter(
        jnp.dot(activated, down_weight, preferred_element_type=jnp.float32),
        "ctx",
        scatter_dimension=0,
        tiled=True,
    )
    return layer_sum.astype(jnp.bfloat16)


def solution(mesh):
    placed = (
        P(("groups", "ctx"), None),
        P(("groups", "ctx"), None),
        P(("groups", "ctx"), None),
        P(("groups", "ctx")),
        P(("groups", "ctx")),
        P(),
        P("ctx", None),
        P("ctx", None),
        P("ctx", None),
    )
    return jax.shard_map(
        local, mesh=mesh, in_specs=placed, out_specs=P(("groups", "ctx"), None), check_vma=False
    )
```

profile of v0, /device:TPU:0, one launch (start us, length us, event | category | flops | bytes accessed | tf_op | source)
XLA Modules:
  0.0 214.6 jit_solution(2000556180046539603)
XLA Ops:
  0.0 1.4 fusion.32
  2.0 0.9 dynamic-update-slice
  2.8 13.7 %all-reduce = s32[32]{0:T(128)S(1)} all-reduce(s32[32]{0:T(128)S(1)} %dynamic-update-slice), channel_id=1, replica_groups=mesh['groups'=2,'ctx'=16] {'ctx'}, use_global_device_ids=true, to_apply=%add | all-reduce | flops 32 | bytes 256
  16.6 0.1 reshape.78
  16.6 19.6 %all-gather = bf16[16,2,8192]{2,1,0:T(2,128)(2,1)S(1)} all-gather(bf16[1,2,8192]{2,1,0:T(2,128)(2,1)} %bitcast.91), channel_id=1, replica_groups=mesh['groups'=2,'ctx'=16] {'ctx'}, dimensions={0}, use_global_device_ids=true | all-gather | bytes 557056 | tf_op jit(solution)/shard_map/all_gather | solution.py:58
  36.3 0.2 reshape.79
  36.5 13.3 %while.14 = (s32[]{:T(128)}, f32[2,16,64]{2,1,0:T(8,128)S(1)}, f32[2,16,64]{2,1,0:T(8,128)S(1)}, f32[2,16,64,128]{3,2,1,0:T(8,128)}, s32[512]{0:T(512)}, /*index...) while((s32[]{:T(128)}, f32[2,16,64]{2,1,0:T(8,128)S(1)}, ...), condition=%wide.region_3.4_spmd, body=%wide.region_0.3_spmd.sunk | while | flops 275257344 | bytes 19778380 | solution.py:67
  36.5 0.8 broadcast_compare_fusion.2
  37.3 1.5 copy.79
  38.8 0.6 bitcast_reduce_fusion.2
  39.5 0.6 copy-done
  40.0 0.3 copy.85
  40.3 0.8 convolution_bitcast_fusion.2
  41.2 0.8 bitcast_dynamic-update-slice_fusion.2
  42.0 0.8 fusion.46
  42.8 0.1 copy.81
  43.0 0.1 copy.84
  43.1 0.8 broadcast_compare_fusion.2
  44.0 1.5 copy.79
  45.5 0.6 bitcast_reduce_fusion.2
  46.1 0.6 copy-done
  46.7 0.3 copy.85
  47.0 0.8 convolution_bitcast_fusion.2
  47.8 0.9 bitcast_dynamic-update-slice_fusion.2
  48.7 0.8 fusion.46
  49.7 0.1 copy.84
  49.8 0.7 reshape.97
  50.5 3.5 %all-to-all-start.1 = ((f32[16,1,128]{2,1,0:T(1,128)}), f32[16,1,128]{2,1,0:T(1,128)S(1)}, u32[]{:S(2)}, u32[]{:S(2)}) async-start(f32[16,1,128]{2,1,0:T(1,128)} %reshape.97), calls=%async_computation.1 | async-start | bytes 16384 | tf_op jit(solution)/shard_map/all_to_all | solution.py:78
  54.0 0.1 reshape.99
  54.1 6.2 %all-to-all-done.1 = f32[16,1,128]{2,1,0:T(1,128)S(1)} async-done(((f32[16,1,128]{2,1,0:T(1,128)}), f32[16,1,128]{2,1,0:T(1,128)S(1)}, u32[]{:S(2)}, u32[]{:S(2)}) %all-to-all-start.1) | async-done | bytes 8224 | tf_op jit(solution)/shard_map/all_to_all | solution.py:78
  60.3 9.0 %all_to_all.15 = f32[16,1,128]{2,1,0:T(1,128)S(1)} all-to-all(f32[16,1,128]{2,1,0:T(1,128)S(1)} %reshape.99), channel_id=1, replica_groups=mesh['groups'=2,'ctx'=16] {'ctx'}, dimensions={0} | all-to-all | bytes 16384 | tf_op jit(solution)/shard_map/all_to_all | solution.py:79
  69.2 3.7 %all-to-all-start = ((f32[16,2,64,128]{3,2,1,0:T(8,128)}), f32[16,2,64,128]{3,2,1,0:T(8,128)S(1)}, u32[]{:S(2)}, u32[]{:S(2)}) async-start(f32[16,2,64,128]{3,2,1,0:T(8,128)} %bitcast.10), calls=%async_computation | async-start | bytes 2097152 | tf_op jit(solution)/shard_map/all_to_all | solution.py:80
  73.6 0.5 broadcast.61
  74.1 0.7 reduce.2
  74.8 0.1 reshape.98
  74.9 0.7 reduce.1
  75.5 0.1 reshape.100
  75.7 20.1 %all-to-all-done = f32[16,2,64,128]{3,2,1,0:T(8,128)S(1)} async-done(((f32[16,2,64,128]{3,2,1,0:T(8,128)}), f32[16,2,64,128]{3,2,1,0:T(8,128)S(1)}, u32[]{:S(2)}, u32[]{:S(2)}) %all-to-all-start) | async-done | bytes 1048608 | tf_op jit(solution)/shard_map/all_to_all | solution.py:80
  95.8 0.3 multiply_reduce_fusion
  96.1 0.1 convert_bitcast_fusion
  96.2 0.1 fusion.26
  96.4 0.1 fusion.30
  96.5 24.1 %all-gather.1 = bf16[16,2,8192]{2,1,0:T(2,128)(2,1)S(1)} all-gather(bf16[1,2,8192]{2,1,0:T(2,128)(2,1)S(1)} %fusion.30), channel_id=1, replica_groups=mesh['groups'=2,'ctx'=16] {'ctx'}, dimensions={0}, use_global_device_ids=true | all-gather | bytes 557056 | tf_op jit(solution)/shard_map/all_gather | solution.py:90
  120.5 0.2 reshape.90
  120.7 9.6 %fusion.33 = f32[32,896]{1,0:T(8,128)S(1)} fusion(bf16[32,8192]{1,0:T(8,128)(2,1)S(1)} %reshape.90, bf16[896,8192]{1,0:T(8,128)(2,1)} %param.17), kind=kOutput, calls=%fused_computation.52 | convolution fusion | flops 469762048 | bytes 15319040 | tf_op jit(solution)/shard_map/dot_general | solution.py:91
  130.3 14.1 %fusion.20 = f32[32,8192]{1,0:T(8,128)S(1)} fusion(bf16[896,8192]{1,0:T(8,128)(2,1)} %param.19, bf16[32,8192]{1,0:T(8,128)(2,1)S(1)} %reshape.90, bf16[896,8192]{1,0:T(8,128)(2,1)} %param.18, f32[32,896]{1,0:T(8,128)S(1)} %fusion.33), kind=kOutput, calls=%fused_computation.31 | convolution fusion | flops 939696128 | bytes 31047680 | tf_op jit(solution)/shard_map/dot_general | solution.py:99
  144.4 69.5 %all-reduce.3 = bf16[32,8192]{1,0:T(8,128)(2,1)S(1)} all-reduce(f32[32,8192]{1,0:T(8,128)S(1)} %fusion.20), channel_id=2, replica_groups=mesh['groups'=2,'ctx'=16] {'ctx'}, use_global_device_ids=true, to_apply=%region_8.9.clone | all-reduce | flops 262144 | bytes 1572864
  213.9 0.7 dynamic-slice_convert_fusion
  (24 shorter events, 0.6 us)
Async XLA Ops:
  38.8 1.2 copy-start
  45.5 1.2 copy-start
  49.8 46.6 %copy-start.1 = (f32[8192]{0:T(1024)S(1)}, f32[8192]{0:T(1024)}, u32[]{:S(2)}) copy-start(f32[8192]{0:T(1024)} %param.16) | copy-start | bytes 98308
  50.5 9.8 %all-to-all-start.1 = ((f32[16,1,128]{2,1,0:T(1,128)}), f32[16,1,128]{2,1,0:T(1,128)S(1)}, u32[]{:S(2)}, u32[]{:S(2)}) async-start(f32[16,1,128]{2,1,0:T(1,128)} %reshape.97), calls=%async_computation.1 | async-start | bytes 16384 | tf_op jit(solution)/shard_map/all_to_all | solution.py:78
  69.2 26.6 %all-to-all-start = ((f32[16,2,64,128]{3,2,1,0:T(8,128)}), f32[16,2,64,128]{3,2,1,0:T(8,128)S(1)}, u32[]{:S(2)}, u32[]{:S(2)}) async-start(f32[16,2,64,128]{3,2,1,0:T(8,128)} %bitcast.10), calls=%async_computation | async-start | bytes 2097152 | tf_op jit(solution)/shard_map/all_to_all | solution.py:80
where the time goes:
time: 215 us
  blocking collectives  136 us (63%)
  matrix products  26.6 us (12%)
  waiting for transfers between devices  26.3 us (12%)
  local copies, waits for them, and re-layouts  12 us (6%)
  starting transfers between devices  7.12 us (3%)
  other arithmetic  5.16 us (2%)
    unnamed x2, blocking collectives  83.3 us
    all_gather x1, blocking collectives, local(): piece = lax.all_gather(normed, 'ctx', axis=0, tiled=True)  24.1 us
    all_to_all x1, waiting for transfers between devices, local(): lax.all_to_all(summed_all, 'ctx', split_axis=0, concat_axis=0, tiled=True)  20.1 us
    all_gather x1, blocking collectives, local(): every_query = lax.all_gather(queries, 'ctx', axis=0, tiled=True)  19.6 us
    dot_general x1, matrix products, local(): jnp.dot(activated, down_weight, preferred_element_type=jnp.float32)  14.1 us
    dot_general x1, matrix products, local(): lax.dot_general(piece, gate_weight, (((1,), (1,)), ((), ())), preferred_e...  9.59 us
    all_to_all x1, blocking collectives, local(): lax.all_to_all(totals_all, 'ctx', split_axis=0, concat_axis=0, tiled=True)  8.97 us
    all_to_all x1, waiting for transfers between devices, local(): lax.all_to_all(peak_all, 'ctx', split_axis=0, concat_axis=0, tiled=True)  6.2 us
  transfers between devices with their start and end apart: 2, of which 2 were waited for; matrix products, arithmetic and copies ran while one was open for 1% of the time, Pallas kernels for 0%

commit v1 on v0

v1 whole, which is shorter than its diff:
```python
import functools

import jax
import jax.numpy as jnp
from jax import lax
from jax.experimental import pallas as pl
from jax.experimental.pallas import tpu as pltpu
from jax.sharding import PartitionSpec as P

KEY_VALUE_HEADS = 8
GROUP = 8
HEAD_SIZE = 128
EPS = 1e-5
PIECES = 4
MESH = pl.DeviceIdType.MESH
bf16, f32 = jnp.bfloat16, jnp.float32


def columns_of(a, first=0):
    return jnp.stack(
        [
            jnp.broadcast_to(a[:, first + g : first + g + 1], (a.shape[0], HEAD_SIZE))
            for g in range(KEY_VALUE_HEADS)
        ]
    )


def kernel(
    n, rows, q_ref, pos_ref, gain_ref, k_hbm, v_hbm, wg_hbm, wu_hbm, wd_hbm, out_ref,
    k_v, v_v, wg, wu, wd, gathq, gathx, part, stats, xs, act,
    pair_send, pair_recv, pst_send, pst_recv, chip_send, chip_recv, cst_send, cst_recv,
    pair2_send, pair2_recv, chip2_send, chip2_recv,
    load_sem, w_sem, ag_send, ag_fwd, ag_recv, pr_send, pr_recv, ch_send, ch_recv,
):
    me = lax.axis_index("ctx")
    half = n // 2
    core = lax.rem(me, 2)
    chip = me // 2
    partner = me + 1 - 2 * core
    chunk = rows * GROUP
    total_rows = n * chunk
    hidden = wg.shape[0]

    k_copy = pltpu.make_async_copy(k_hbm, k_v, load_sem.at[0])
    v_copy = pltpu.make_async_copy(v_hbm, v_v, load_sem.at[1])
    k_copy.start()
    v_copy.start()
    w_copies = []
    step = hidden // PIECES // 16 * 16
    for i, (src, dst) in enumerate(((wg_hbm, wg), (wu_hbm, wu), (wd_hbm, wd))):
        for j in range(PIECES):
            size = step if j < PIECES - 1 else hidden - step * (PIECES - 1)
            span = pl.ds(j * step, size)
            w_copies.append(
                pltpu.make_async_copy(src.at[span], dst.at[span], w_sem.at[i, j])
            )

    def remote(src, dst, send, recv, to):
        return pltpu.make_async_remote_copy(
            src_ref=src, dst_ref=dst, send_sem=send, recv_sem=recv,
            device_id={"ctx": to}, device_id_type=MESH,
        )

    def loop(lo, hi, body):
        def step(i, carry):
            body(i)
            return carry

        lax.fori_loop(lo, hi, step, 0)

    barrier = pltpu.get_barrier_semaphore()
    pl.semaphore_signal(barrier, inc=1, device_id={"ctx": partner}, device_id_type=MESH)

    def greet(k):
        to = 2 * lax.rem(chip + k, half) + core
        pl.semaphore_signal(barrier, inc=1, device_id={"ctx": to}, device_id_type=MESH)

    loop(1, half, greet)
    gathq[me] = q_ref[...]
    pl.semaphore_wait(barrier, half)

    def gather(buf, which, during=None):
        def copy_to(source, to, send):
            return remote(buf.at[source], buf.at[source], send, ag_recv.at[which, source], to)

        def send(k):
            copy_to(me, 2 * lax.rem(chip + k, half) + core, ag_send.at[which, k]).start()

        copy_to(me, partner, ag_send.at[which, 0]).start()
        loop(1, half, send)
        if during is not None:
            during()

        def forward(k):
            source = 2 * lax.rem(chip + half - k, half) + core
            copy_to(source, partner, ag_fwd.at[which, k]).wait_recv()
            copy_to(source, partner, ag_fwd.at[which, k]).start()

        loop(1, half, forward)

        def arrive(p):
            copy_to(2 * p + 1 - core, partner, ag_send.at[which, 0]).wait_recv()

        loop(0, half, arrive)

        def sent(k):
            copy_to(me, partner, ag_send.at[which, k]).wait_send()

        loop(0, half, sent)

        def forwarded(k):
            source = 2 * lax.rem(chip + half - k, half) + core
            copy_to(source, partner, ag_fwd.at[which, k]).wait_send()

        loop(1, half, forwarded)

    def start_weights():
        for copy in w_copies:
            copy.start()

    gather(gathq, 0, start_weights)

    k_copy.wait()
    v_copy.wait()
    limits = gathq[:, KEY_VALUE_HEADS].reshape(total_rows, HEAD_SIZE).astype(f32)
    limit = limits[:, 0:1] * 256.0 + limits[:, 64:65]
    live = pos_ref[...].astype(f32) < limit
    lane = lax.broadcasted_iota(jnp.int32, (total_rows, HEAD_SIZE), 1)
    stats[...] = jnp.zeros_like(stats)

    def head(g):
        span = pl.ds(pl.multiple_of(g * HEAD_SIZE, HEAD_SIZE), HEAD_SIZE)
        q = gathq[:, g].reshape(total_rows, HEAD_SIZE)
        s = lax.dot_general(
            q, k_v[:, span], (((1,), (1,)), ((), ())), preferred_element_type=f32
        ) * HEAD_SIZE ** (-0.5)
        s = jnp.where(live, s, -1e30)
        m = jnp.max(s, axis=1, keepdims=True)
        w = jnp.where(live, jnp.exp(s - m), 0.0)
        t = jnp.sum(w, axis=1, keepdims=True)
        part[g] = jnp.dot(w.astype(bf16), v_v[:, span], preferred_element_type=f32)
        stats[...] = jnp.where(lane == g, m, jnp.where(lane == 64 + g, t, stats[...]))

    loop(0, KEY_VALUE_HEADS, head)

    small = lax.broadcasted_iota(jnp.int32, (chunk, HEAD_SIZE), 1)

    def slab(d):
        return pl.ds(pl.multiple_of(d * chunk, chunk), chunk)

    def pair_copy(which, p):
        src, dst = ((pair_send, pair_recv), (pst_send, pst_recv), (pair2_send, pair2_recv))[which]
        return remote(src.at[p], dst.at[p], pr_send.at[which, p], pr_recv.at[which, p], partner)

    def chip_copy(which, p, slot):
        src, dst = ((chip_send, chip_recv), (cst_send, cst_recv), (chip2_send, chip2_recv))[which]
        return remote(
            src.at[p], dst.at[slot], ch_send.at[which, p], ch_recv.at[which, slot], 2 * p + core
        )

    def to_pair(j):
        p = lax.rem(chip + 1 + j, half)
        d = 2 * p + 1 - core
        pst_send[p] = stats[slab(d), :]
        pair_copy(1, p).start()
        pair_send[p] = part[:, slab(d), :].astype(bf16)
        pair_copy(0, p).start()

    loop(0, half, to_pair)

    def merge(p):
        d = 2 * p + core
        pair_copy(1, p).wait_recv()
        s1, s2 = stats[slab(d), :], pst_recv[p]
        m = jnp.maximum(s1, s2)
        a1, a2 = jnp.exp(s1 - m), jnp.exp(s2 - m)
        t = s1 * pltpu.roll(a1, 64, 1) + s2 * pltpu.roll(a2, 64, 1)
        pair_copy(0, p).wait_recv()
        summed = part[:, slab(d), :] * columns_of(a1) + pair_recv[p].astype(f32) * columns_of(a2)
        return jnp.where(small < 64, m, t), summed.astype(bf16)

    def to_owner(j):
        p = lax.rem(chip + 1 + j, half)
        state, summed = merge(p)
        cst_send[p] = state
        chip_copy(1, p, chip).start()
        chip_send[p] = summed
        chip_copy(0, p, chip).start()

    loop(0, half - 1, to_owner)
    state, summed = merge(chip)
    cst_recv[chip] = state
    chip_recv[chip] = summed

    def settle(which):
        def body(k):
            p = lax.rem(chip + half - k, half)
            chip_copy(which, p, p).wait_recv()

        return body

    loop(1, half, settle(1))
    loop(1, half, settle(0))
    peak = jnp.max(cst_recv[...], axis=0)

    def add(p, carry):
        totals, acc = carry
        s = cst_recv[p]
        a = jnp.exp(s - peak)
        totals = totals + s * pltpu.roll(a, 64, 1)
        return totals, acc + chip_recv[p].astype(f32) * columns_of(a)

    totals, acc = lax.fori_loop(
        0, half, add,
        (jnp.zeros((chunk, HEAD_SIZE), f32), jnp.zeros((KEY_VALUE_HEADS, chunk, HEAD_SIZE), f32)),
    )
    wide = (acc / columns_of(totals, 64)).astype(bf16).astype(f32)
    squares = jnp.sum(jnp.sum(wide * wide, axis=0), axis=1, keepdims=True)
    features = KEY_VALUE_HEADS * GROUP * HEAD_SIZE
    scale = jnp.concatenate(
        [
            jnp.broadcast_to(
                lax.rsqrt(
                    jnp.sum(squares[r * GROUP : (r + 1) * GROUP], axis=0, keepdims=True) / features
                    + EPS
                ),
                (GROUP, HEAD_SIZE),
            )
            for r in range(rows)
        ],
        axis=0,
    )
    gain = jnp.concatenate([gain_ref[...]] * rows, axis=1)
    gathx[me] = (wide * scale[None] * gain).astype(bf16)

    def finish_sends(which):
        loop(0, half, lambda p: pair_copy(which, p).wait_send())
        loop(1, half, lambda k: chip_copy(which, lax.rem(chip + k, half), chip).wait_send())

    gather(gathx, 1, lambda: (finish_sends(0), finish_sends(1)))

    def widen(d):
        part[:, slab(d), :] = gathx[d].astype(f32)

    loop(0, n, widen)

    def spread(g):
        for h in range(GROUP):
            span = pl.ds(pl.multiple_of((g * GROUP + h) * HEAD_SIZE, HEAD_SIZE), HEAD_SIZE)
            xs[:, span] = part[g, pl.ds(h, n * rows, stride=GROUP), :].astype(bf16)

    loop(0, KEY_VALUE_HEADS, spread)

    for copy in w_copies[: 2 * PIECES]:
        copy.wait()
    first = 0
    while first < hidden:
        size = min(256, hidden - first)
        contract = (((1,), (1,)), ((), ()))
        gate = lax.dot_general(xs[...], wg[first : first + size, :], contract, preferred_element_type=f32)
        up = lax.dot_general(xs[...], wu[first : first + size, :], contract, preferred_element_type=f32)
        act[:, first : first + size] = (gate / (1.0 + jnp.exp(-gate)) * up).astype(bf16)
        first += size
    for copy in w_copies[2 * PIECES :]:
        copy.wait()

    def down(g):
        width = GROUP * HEAD_SIZE
        o = jnp.dot(
            act[...], wd[:, pl.ds(pl.multiple_of(g * width, width), width)],
            preferred_element_type=f32,
        )
        for h in range(GROUP):
            part[g, pl.ds(h, n * rows, stride=GROUP), :] = o[:, h * HEAD_SIZE : (h + 1) * HEAD_SIZE]

    loop(0, KEY_VALUE_HEADS, down)

    def to_pair2(j):
        p = lax.rem(chip + 1 + j, half)
        pair2_send[p] = part[:, slab(2 * p + 1 - core), :].astype(bf16)
        pair_copy(2, p).start()

    loop(0, half, to_pair2)

    def merge2(p):
        pair_copy(2, p).wait_recv()
        return part[:, slab(2 * p + core), :] + pair2_recv[p].astype(f32)

    def to_owner2(j):
        p = lax.rem(chip + 1 + j, half)
        chip2_send[p] = merge2(p).astype(bf16)
        chip_copy(2, p, chip).start()

    loop(0, half - 1, to_owner2)
    mine = merge2(chip)

    def add2(k, acc):
        p = lax.rem(chip + half - k, half)
        chip_copy(2, p, p).wait_recv()
        return acc + chip2_recv[p].astype(f32)

    out_ref[...] = lax.fori_loop(1, half, add2, mine).astype(bf16)
    finish_sends(2)


def local(queries, keys, values, position, lengths, gain, gate_weight, up_weight, down_weight):
    n = lax.axis_size("ctx")
    half = n // 2
    rows, width = queries.shape
    slots, kv_width = keys.shape
    hidden = gate_weight.shape[0]
    chunk = rows * GROUP
    q = queries.reshape(rows, KEY_VALUE_HEADS, GROUP, HEAD_SIZE).transpose(1, 0, 2, 3)
    q = q.reshape(KEY_VALUE_HEADS, chunk, HEAD_SIZE)
    spread = jnp.broadcast_to(lengths[:, None, None], (rows, GROUP, 64)).reshape(1, chunk, 64)
    coded = jnp.concatenate([spread // 256, spread % 256], axis=2).astype(bf16)
    q = jnp.concatenate([q, coded], axis=0)

    block = (KEY_VALUE_HEADS, chunk, HEAD_SIZE)
    vm = pltpu.VMEM
    data = lambda: vm((half,) + block, bf16)
    state = lambda: vm((half, chunk, HEAD_SIZE), f32)
    dma = pltpu.SemaphoreType.DMA
    in_vmem = pl.BlockSpec(memory_space=pltpu.VMEM)
    in_hbm = pl.BlockSpec(memory_space=pl.ANY)
    out = pl.pallas_call(
        functools.partial(kernel, n, rows),
        out_shape=jax.ShapeDtypeStruct(block, bf16),
        in_specs=[in_vmem] * 3 + [in_hbm] * 5,
        out_specs=in_vmem,
        scratch_shapes=[
            vm((slots, kv_width), bf16),
            vm((slots, kv_width), bf16),
            vm((hidden, width), bf16),
            vm((hidden, width), bf16),
            vm((hidden, width), bf16),
            vm((n, KEY_VALUE_HEADS + 1, chunk, HEAD_SIZE), bf16),
            vm((n,) + block, bf16),
            vm((KEY_VALUE_HEADS, n * chunk, HEAD_SIZE), f32),
            vm((n * chunk, HEAD_SIZE), f32),
            vm((n * rows, width), bf16),
            vm((n * rows, hidden), bf16),
            data(), data(), state(), state(),
            data(), data(), state(), state(),
            data(), data(), data(), data(),
            dma((2,)), dma((3, PIECES)),
            dma((2, half)), dma((2, half)), dma((2, n)),
            dma((3, half)), dma((3, half)), dma((3, half)), dma((3, half)),
        ],
        compiler_params=pltpu.CompilerParams(
            collective_id=0, has_side_effects=True, vmem_limit_bytes=60 * 2**20
        ),
    )(
        q, position.reshape(1, slots), gain.reshape(KEY_VALUE_HEADS, GROUP, HEAD_SIZE),
        keys, values, gate_weight, up_weight, down_weight,
    )
    out = out.reshape(KEY_VALUE_HEADS, rows, GROUP, HEAD_SIZE).transpose(1, 0, 2, 3)
    return out.reshape(rows, width)


def solution(mesh):
    split = P(("groups", "ctx"))
    tall = P(("groups", "ctx"), None)
    weight = P("ctx", None)
    return jax.shard_map(
        local,
        mesh=mesh,
        in_specs=(tall, tall, tall, split, split, P(), weight, weight, weight),
        out_specs=tall,
        check_vma=False,
    )
```

time: 215 us -> 64 us (0.30)
  blocking collectives: 136 us -> 0 us
  Pallas kernels: 0 us -> 59.9 us
  matrix products: 26.6 us -> 0 us
  waiting for transfers between devices: 26.3 us -> 0 us
  local copies, waits for them, and re-layouts: 12 us -> 2.99 us
  starting transfers between devices: 7.12 us -> 0 us
  other arithmetic: 5.16 us -> 0.79 us
    unnamed x2 -> x0, blocking collectives: 83.3 us -> none
    pallas_call x0 -> x1, Pallas kernels: none -> 59.9 us  [local(): pl.pallas_call(functools.partial(kernel, n, rows), out_shape=jax.ShapeDty...]
    all_gather x2 -> x0, blocking collectives: 43.7 us -> none  [the longest x1 24.1 us: local(): piece = lax.all_gather(normed, 'ctx', axis=0, tiled=True)]
    dot_general x6 -> x0, matrix products: 26.6 us -> none  [the longest x1 14.1 us: local(): jnp.dot(activated, down_weight, preferred_element_type=jnp.float32)]
    all_to_all x2 -> x0, waiting for transfers between devices: 26.3 us -> none  [the longest x1 20.1 us: local(): lax.all_to_all(summed_all, 'ctx', split_axis=0, concat_axis=0, tiled=True)]
    all_to_all x1 -> x0, blocking collectives: 8.97 us -> none  [local(): lax.all_to_all(totals_all, 'ctx', split_axis=0, concat_axis=0, tiled=True)]
    all_to_all x2 -> x0, starting transfers between devices: 7.12 us -> none  [the longest x1 3.65 us: local(): lax.all_to_all(summed_all, 'ctx', split_axis=0, concat_axis=0, tiled=True)]
    while x12 -> x0, local copies, waits for them, and re-layouts: 4.81 us -> none
  transfers between devices with their start and end apart: 2 -> 0, of which waited for: 2 -> 0; matrix products, arithmetic and copies ran while one was open for 1% -> 0% of each run, Pallas kernels for 0% -> 0%
where the time goes in v1:
time: 64 us; the launch traced here: 63.7 us
  Pallas kernels  59.9 us (94%)
  local copies, waits for them, and re-layouts  2.99 us (5%)
  other arithmetic  0.79 us (1%)
    pallas_call x1, Pallas kernels, local(): pl.pallas_call(functools.partial(kernel, n, rows), out_shape=jax.ShapeDty...  59.9 us
    unnamed x2, local copies, waits for them, and re-layouts  1.41 us

profile of v1, /device:TPU:0, one launch (start us, length us, event | category | flops | bytes accessed | tf_op | source)
XLA Modules:
  0.0 63.7 jit_solution(1737819099684834769)
XLA Ops:
  0.0 0.7 %broadcast_in_dim.22 = s32[2,8]{1,0:T(2,128)S(1)} broadcast(s32[2]{0:T(128)} %param.13), dimensions={0} | broadcast | bytes 72 | tf_op jit(solution)/shard_map/broadcast_in_dim | solution.py:315
  0.7 0.1 broadcast_in_dim.23
  0.8 0.1 fusion.3
  0.9 0.8 %copy_bitcast_fusion.3 = bf16[8,16,128]{2,1,0:T(8,128)(2,1)S(1)} fusion(bf16[1,2,64,128]{3,1,2,0:T(2,128)(2,1)} %bitcast.26), kind=kLoop, calls=%fused_computation.4 | loop fusion | bytes 65536 | tf_op jit(solution)/shard_map/reshape | solution.py:314
  1.7 0.7 %maximum_maximum_fusion.q_ref = bf16[9,16,128]{2,1,0:T(8,128)(2,1)} fusion(bf16[1,16,64]{2,1,0:T(8,128)(2,1)S(1)} %get-tuple-element.10, bf16[1,16,64]{2,1,0:T(8,128)(2,1)S(1)} %get-tuple-element.9, bf16[8,16,128]{2,1,0:T(8,128)(2,1)S(1)} %copy_bitcast_fusion.3), kind=kLoop, calls=%fused_computation | loop fusion | flops 110592 | bytes 73728 | tf_op jit(solution)/shard_map/concatenate | solution.py:317
  2.4 59.9 %shard_map.91 = bf16[8,16,128]{2,1,0:T(8,128)(2,1)} custom-call(bf16[9,16,128]{2,1,0:T(8,128)(2,1)} %maximum_maximum_fusion.q_ref, s32[1,512]{1,0:T(1,128)} %bitcast.28, f32[8,8,128]{2,1,0:T(8,128)} %bitcast.27, bf16[512,1024]{1,0:T(8,128)(2,1)} %k_hbm.1, bf16[512,1024]{1,0:T(8,128)(2,1)} %v_hbm.1, bf16[896,8192]{1,0:T(8,128)(2,1)} %wg_hbm.1, ...), custom_call_target="tpu_custom_call" | custom-call | tf_op jit(solution)/shard_map/pallas_call | solution.py:326
  62.3 0.8 %copy_bitcast_fusion.2 = bf16[1,2,64,128]{3,2,1,0:T(8,128)(2,1)S(1)} fusion(bf16[8,16,128]{2,1,0:T(8,128)(2,1)} %shard_map.91), kind=kLoop, calls=%fused_computation.3 | loop fusion | bytes 65536
  63.0 0.6 %copy.19 = bf16[1,2,64,128]{3,1,2,0:T(2,128)(2,1)} copy(bf16[1,2,64,128]{3,2,1,0:T(8,128)(2,1)S(1)} %copy_bitcast_fusion.2) | data formatting | bytes 65536
  (3 shorter events, 0.0 us)

commit v2 on v1

v2 whole, which is shorter than its diff:
```python
import functools

import jax
import jax.numpy as jnp
from jax import lax
from jax.experimental import pallas as pl
from jax.experimental.pallas import tpu as pltpu
from jax.sharding import PartitionSpec as P

KEY_VALUE_HEADS = 8
GROUP = 8
HEAD_SIZE = 128
EPS = 1e-5
PIECES = 4
MESH = pl.DeviceIdType.MESH
bf16, f32 = jnp.bfloat16, jnp.float32


def kernel(
    n, rows, len_ref, q_ref, pos_ref, gain_ref, k_hbm, v_hbm, wg_hbm, wu_hbm, wd_hbm, out_ref,
    k_v, v_v, wg, wu, wd, gathq, gathx, part, stats, square, gate_sum, up_sum, act, turn,
    pair_send, pair_recv, pst_send, pst_recv, chip_send, chip_recv, cst_send, cst_recv,
    pair2_send, pair2_recv, chip2_send, chip2_recv,
    load_sem, w_sem, ag_send, ag_fwd, ag_recv, pr_send, pr_recv, ch_send, ch_recv,
):
    me = lax.axis_index("ctx")
    half = n // 2
    core = lax.rem(me, 2)
    chip = me // 2
    partner = me + 1 - 2 * core
    chunk = rows * GROUP
    hidden = wg.shape[0]

    k_copy = pltpu.make_async_copy(k_hbm, k_v, load_sem.at[0])
    v_copy = pltpu.make_async_copy(v_hbm, v_v, load_sem.at[1])
    k_copy.start()
    v_copy.start()
    w_copies = []
    step = hidden // PIECES // 16 * 16
    for i, (src, dst) in enumerate(((wg_hbm, wg), (wu_hbm, wu), (wd_hbm, wd))):
        for j in range(PIECES):
            size = step if j < PIECES - 1 else hidden - step * (PIECES - 1)
            span = pl.ds(j * step, size)
            w_copies.append(
                pltpu.make_async_copy(src.at[span], dst.at[span], w_sem.at[i, j])
            )

    def remote(src, dst, send, recv, to):
        return pltpu.make_async_remote_copy(
            src_ref=src, dst_ref=dst, send_sem=send, recv_sem=recv,
            device_id={"ctx": to}, device_id_type=MESH,
        )

    def loop(lo, hi, body):
        def step(i, carry):
            body(i)
            return carry

        lax.fori_loop(lo, hi, step, 0)

    barrier = pltpu.get_barrier_semaphore()
    pl.semaphore_signal(barrier, inc=1, device_id={"ctx": partner}, device_id_type=MESH)

    def greet(k):
        to = 2 * lax.rem(chip + k, half) + core
        pl.semaphore_signal(barrier, inc=1, device_id={"ctx": to}, device_id_type=MESH)

    loop(1, half, greet)
    q = q_ref[...].astype(f32)
    for g in range(KEY_VALUE_HEADS):
        for h in range(GROUP):
            first = (g * GROUP + h) * HEAD_SIZE
            turn[g, pl.ds(h, rows, stride=GROUP), :] = q[:, first : first + HEAD_SIZE]
    gathq[me, :KEY_VALUE_HEADS] = turn[...].astype(bf16)
    low = lax.broadcasted_iota(jnp.int32, (GROUP, HEAD_SIZE), 1) < 64
    coded = [jnp.where(low, len_ref[r] >> 8, len_ref[r] & 255) for r in range(rows)]
    gathq[me, KEY_VALUE_HEADS] = jnp.concatenate(coded, axis=0).astype(f32).astype(bf16)
    pl.semaphore_wait(barrier, half)

    def gather_copy(which, source, to, send):
        buf = (gathq, gathx)[which]
        return remote(buf.at[source], buf.at[source], send, ag_recv.at[which, source], to)

    def source_of(k):
        return lax.rem(chip + half - k, half)

    def gather_start(which):
        def send(k):
            to = 2 * lax.rem(chip + k, half) + core
            gather_copy(which, me, to, ag_send.at[which, k]).start()

        gather_copy(which, me, partner, ag_send.at[which, 0]).start()
        loop(1, half, send)

    def forward(which, k):
        source = 2 * source_of(k) + core
        gather_copy(which, source, partner, ag_fwd.at[which, k]).wait_recv()
        gather_copy(which, source, partner, ag_fwd.at[which, k]).start()

    def arrive(which, p):
        gather_copy(which, 2 * p + 1 - core, partner, ag_send.at[which, 0]).wait_recv()

    def gather_end(which):
        loop(0, half, lambda k: gather_copy(which, me, partner, ag_send.at[which, k]).wait_send())

        def forwarded(k):
            source = 2 * source_of(k) + core
            gather_copy(which, source, partner, ag_fwd.at[which, k]).wait_send()

        loop(1, half, forwarded)

    gather_start(0)
    for copy in w_copies:
        copy.start()
    loop(1, half, lambda k: forward(0, k))
    loop(0, half, lambda p: arrive(0, p))

    def slab(d):
        return pl.ds(pl.multiple_of(d * chunk, chunk), chunk)

    every = n * rows
    own_heads = KEY_VALUE_HEADS * GROUP // n
    block = own_heads * every
    shared = half // KEY_VALUE_HEADS

    def widen(d):
        part[:, slab(d), :] = gathq[d, :KEY_VALUE_HEADS].astype(f32)
        stats[0, slab(d), :] = gathq[d, KEY_VALUE_HEADS].astype(f32)

    loop(0, n, widen)
    limits = stats[0, pl.ds(0, every, stride=GROUP), :]
    limit = jnp.concatenate([limits[:, 0:1] * 256.0 + limits[:, 64:65]] * GROUP, axis=0)
    live = pos_ref[...].astype(f32) < limit
    lane = lax.broadcasted_iota(jnp.int32, (GROUP * every, HEAD_SIZE), 1)
    small = lax.broadcasted_iota(jnp.int32, (block, HEAD_SIZE), 1)
    k_copy.wait()
    v_copy.wait()

    def pair_copy(which, p):
        src, dst = ((pair_send, pair_recv), (pst_send, pst_recv), (pair2_send, pair2_recv))[which]
        return remote(src.at[p], dst.at[p], pr_send.at[which, p], pr_recv.at[which, p], partner)

    def chip_copy(which, p, slot):
        src, dst = ((chip_send, chip_recv), (cst_send, cst_recv), (chip2_send, chip2_recv))[which]
        return remote(
            src.at[p], dst.at[slot], ch_send.at[which, p], ch_recv.at[which, slot], 2 * p + core
        )

    def head_at(j):
        return lax.rem(chip // shared + 1 + j, KEY_VALUE_HEADS)

    def rows_of(i):
        return pl.ds(pl.multiple_of(i * block, block), block)

    def merge(j):
        g = head_at(j)
        for i in range(shared):
            p = g * shared + i
            span = rows_of(2 * i + core)
            pair_copy(1, p).wait_recv()
            theirs = jnp.transpose(pst_recv[p])
            m1, t1 = stats[g, span, 0:1], stats[g, span, 4:5]
            m2, t2 = theirs[:, 0:1], theirs[:, 4:5]
            m = jnp.maximum(m1, m2)
            a1, a2 = jnp.exp(m1 - m), jnp.exp(m2 - m)
            state = jnp.transpose(jnp.where(small < 4, m, t1 * a1 + t2 * a2))[0:8]
            pair_copy(0, p).wait_recv()
            summed = (part[g, span, :] * a1 + pair_recv[p].astype(f32) * a2).astype(bf16)

            @pl.when(p == chip)
            def _():
                cst_recv[chip] = state
                chip_recv[chip] = summed

            @pl.when(p != chip)
            def _():
                cst_send[p] = state
                chip_copy(1, p, chip).start()
                chip_send[p] = summed
                chip_copy(0, p, chip).start()

    def head(j):
        g = head_at(j)
        span = pl.ds(pl.multiple_of(g * HEAD_SIZE, HEAD_SIZE), HEAD_SIZE)
        q = jnp.concatenate(
            [part[g, pl.ds(h, every, stride=GROUP), :] for h in range(GROUP)], axis=0
        ).astype(bf16)
        s = lax.dot_general(
            q, k_v[:, span], (((1,), (1,)), ((), ())), preferred_element_type=f32
        ) * HEAD_SIZE ** (-0.5)
        s = jnp.where(live, s, -1e30)
        m = jnp.max(s, axis=1, keepdims=True)
        w = jnp.where(live, jnp.exp(s - m), 0.0)
        t = jnp.sum(w, axis=1, keepdims=True)
        part[g] = jnp.dot(w.astype(bf16), v_v[:, span], preferred_element_type=f32)
        stats[g] = jnp.where(lane < 4, m, t)
        for i in range(shared):
            p = g * shared + i
            theirs = rows_of(2 * i + 1 - core)
            pst_send[p] = jnp.transpose(stats[g, theirs, :])[0:8]
            pair_copy(1, p).start()
            pair_send[p] = part[g, theirs, :].astype(bf16)
            pair_copy(0, p).start()

        @pl.when(j > 0)
        def _():
            merge(j - 1)

    loop(0, KEY_VALUE_HEADS, head)
    merge(KEY_VALUE_HEADS - 1)

    def settle(k):
        p = source_of(k)
        chip_copy(1, p, p).wait_recv()
        chip_copy(0, p, p).wait_recv()

    loop(1, half, settle)
    peaks, totals = cst_recv[:, 0, :], cst_recv[:, 4, :]
    factor = jnp.exp(peaks - jnp.max(peaks, axis=0, keepdims=True))
    factor = factor / jnp.sum(factor * totals, axis=0, keepdims=True)
    factor = jnp.transpose(factor)
    attended = jnp.zeros((block, HEAD_SIZE), f32)
    for p in range(half):
        attended = attended + chip_recv[p].astype(f32) * factor[:, p : p + 1]
    attended = attended.astype(bf16)
    gathx[me] = jnp.concatenate(
        [attended[i * every : (i + 1) * every] for i in range(own_heads)], axis=1
    )

    def finish_sends(which):
        loop(0, half, lambda p: pair_copy(which, p).wait_send())
        loop(1, half, lambda k: chip_copy(which, lax.rem(chip + k, half), chip).wait_send())

    gather_start(1)
    gather_end(0)
    finish_sends(0)
    finish_sends(1)
    for copy in w_copies[: 2 * PIECES]:
        copy.wait()
    square[...] = jnp.zeros_like(square)
    gate_sum[...] = jnp.zeros_like(gate_sum)
    up_sum[...] = jnp.zeros_like(up_sum)
    deep = 2 * own_heads * HEAD_SIZE

    def products(p):
        x = jnp.concatenate([gathx[2 * p], gathx[2 * p + 1]], axis=1).astype(f32)
        span = pl.ds(pl.multiple_of(p * deep, deep), deep)
        total = square[...]
        for i in range(2 * own_heads):
            piece = x[:, i * HEAD_SIZE : (i + 1) * HEAD_SIZE]
            total = total + piece * piece
        square[...] = total
        scaled = (x * gain_ref[:, span]).astype(bf16)
        contract = (((1,), (1,)), ((), ()))
        first = 0
        while first < hidden:
            size = min(256, hidden - first)
            cut = slice(first, first + size)
            gate_sum[:, cut] += lax.dot_general(
                scaled, wg[cut, span], contract, preferred_element_type=f32
            )
            up_sum[:, cut] += lax.dot_general(
                scaled, wu[cut, span], contract, preferred_element_type=f32
            )
            first += size

    forward(1, 1)
    arrive(1, chip)
    products(chip)

    def next_chip(k):
        @pl.when(k + 1 < half)
        def _():
            forward(1, k + 1)

        arrive(1, source_of(k))
        products(source_of(k))

    loop(1, half, next_chip)
    features = KEY_VALUE_HEADS * GROUP * HEAD_SIZE
    scale = lax.rsqrt(jnp.sum(square[...], axis=1, keepdims=True) / features + EPS)
    gate = gate_sum[...] * scale
    act[...] = (gate / (1.0 + jnp.exp(-gate)) * (up_sum[...] * scale)).astype(bf16)
    gather_end(1)
    for copy in w_copies[2 * PIECES :]:
        copy.wait()

    def down(g):
        width = GROUP * HEAD_SIZE
        o = jnp.dot(
            act[...], wd[:, pl.ds(pl.multiple_of(g * width, width), width)],
            preferred_element_type=f32,
        )
        for h in range(GROUP):
            part[g, pl.ds(h, n * rows, stride=GROUP), :] = o[:, h * HEAD_SIZE : (h + 1) * HEAD_SIZE]

    loop(0, KEY_VALUE_HEADS, down)

    def to_pair2(j):
        p = lax.rem(chip + 1 + j, half)
        pair2_send[p] = part[:, slab(2 * p + 1 - core), :].astype(bf16)
        pair_copy(2, p).start()

    loop(0, half, to_pair2)

    def merge2(p):
        pair_copy(2, p).wait_recv()
        return part[:, slab(2 * p + core), :] + pair2_recv[p].astype(f32)

    def to_owner2(j):
        p = lax.rem(chip + 1 + j, half)
        chip2_send[p] = merge2(p).astype(bf16)
        chip_copy(2, p, chip).start()

    loop(0, half - 1, to_owner2)
    mine = merge2(chip)

    def add2(k, acc):
        p = lax.rem(chip + half - k, half)
        chip_copy(2, p, p).wait_recv()
        return acc + chip2_recv[p].astype(f32)

    turn[...] = lax.fori_loop(1, half, add2, mine)
    out_ref[...] = jnp.concatenate(
        [
            turn[g, pl.ds(h, rows, stride=GROUP), :]
            for g in range(KEY_VALUE_HEADS)
            for h in range(GROUP)
        ],
        axis=1,
    ).astype(bf16)
    finish_sends(2)


def local(queries, keys, values, position, lengths, gain, gate_weight, up_weight, down_weight):
    n = lax.axis_size("ctx")
    half = n // 2
    rows, width = queries.shape
    slots, kv_width = keys.shape
    hidden = gate_weight.shape[0]
    chunk = rows * GROUP
    own = KEY_VALUE_HEADS * GROUP // n
    every = n * rows
    block = (KEY_VALUE_HEADS, chunk, HEAD_SIZE)
    vm = pltpu.VMEM
    data = lambda: vm((half,) + block, bf16)
    state = lambda: vm((half, 8, HEAD_SIZE), f32)
    heads = lambda: vm((half, own * every, HEAD_SIZE), bf16)
    dma = pltpu.SemaphoreType.DMA
    in_vmem = pl.BlockSpec(memory_space=pltpu.VMEM)
    in_hbm = pl.BlockSpec(memory_space=pl.ANY)
    return pl.pallas_call(
        functools.partial(kernel, n, rows),
        out_shape=jax.ShapeDtypeStruct((rows, width), bf16),
        in_specs=[pl.BlockSpec(memory_space=pltpu.SMEM)] + [in_vmem] * 3 + [in_hbm] * 5,
        out_specs=in_vmem,
        scratch_shapes=[
            vm((slots, kv_width), bf16),
            vm((slots, kv_width), bf16),
            vm((hidden, width), bf16),
            vm((hidden, width), bf16),
            vm((hidden, width), bf16),
            vm((n, KEY_VALUE_HEADS + 1, chunk, HEAD_SIZE), bf16),
            vm((n, every, own * HEAD_SIZE), bf16),
            vm((KEY_VALUE_HEADS, n * chunk, HEAD_SIZE), f32),
            vm((KEY_VALUE_HEADS, n * chunk, HEAD_SIZE), f32),
            vm((every, HEAD_SIZE), f32),
            vm((every, hidden), f32),
            vm((every, hidden), f32),
            vm((every, hidden), bf16),
            vm(block, f32),
            heads(), heads(), state(), state(),
            heads(), heads(), state(), state(),
            data(), data(), data(), data(),
            dma((2,)), dma((3, PIECES)),
            dma((2, half)), dma((2, half)), dma((2, n)),
            dma((3, half)), dma((3, half)), dma((3, half)), dma((3, half)),
        ],
        compiler_params=pltpu.CompilerParams(
            collective_id=0, has_side_effects=True, vmem_limit_bytes=60 * 2**20
        ),
    )(
        lengths, queries, position.reshape(1, slots), gain.reshape(1, width),
        keys, values, gate_weight, up_weight, down_weight,
    )


def solution(mesh):
    split = P(("groups", "ctx"))
    tall = P(("groups", "ctx"), None)
    weight = P("ctx", None)
    return jax.shard_map(
        local,
        mesh=mesh,
        in_specs=(tall, tall, tall, split, split, P(), weight, weight, weight),
        out_specs=tall,
        check_vma=False,
    )
```

time: 64 us -> 57.9 us (0.905)
  Pallas kernels: 59.9 us -> 56.2 us
  local copies, waits for them, and re-layouts: 2.99 us -> 1.4 us
  other arithmetic: 0.79 us -> 0 us
    pallas_call x1, Pallas kernels: 59.9 us -> 56.2 us  [local(): pl.pallas_call(functools.partial(kernel, n, rows), out_shape=jax.ShapeDty...]
    broadcast_in_dim x2 -> x0, local copies, waits for them, and re-layouts: 0.81 us -> none  [local(): jnp.broadcast_to(lengths[:, None, None], (rows, GROUP, 64))]
    concatenate x2 -> x0, other arithmetic: 0.77 us -> none  [the longest x1 0.69 us: local(): q = jnp.concatenate([q, coded], axis=0)]
    reshape x1 -> x0, local copies, waits for them, and re-layouts: 0.77 us -> none  [local(): q = q.reshape(KEY_VALUE_HEADS, chunk, HEAD_SIZE)]
    unnamed x2 -> x1, local copies, waits for them, and re-layouts: 1.41 us -> 1.4 us
where the time goes in v2:
time: 57.9 us; the launch traced here: 57.6 us
  Pallas kernels  56.2 us (97%)
  local copies, waits for them, and re-layouts  1.4 us (2%)
    pallas_call x1, Pallas kernels, local(): pl.pallas_call(functools.partial(kernel, n, rows), out_shape=jax.ShapeDty...  56.2 us
    unnamed x1, local copies, waits for them, and re-layouts  1.4 us

profile of v2, /device:TPU:0, one launch (start us, length us, event | category | flops | bytes accessed | tf_op | source)
XLA Modules:
  0.0 57.6 jit_solution(5917901198567090685)
XLA Ops:
  0.0 56.2 %shard_map.91 = bf16[2,8192]{1,0:T(2,128)(2,1)} custom-call(s32[2]{0:T(128)} %len_ref.1, bf16[2,8192]{1,0:T(2,128)(2,1)} %q_ref.1, s32[1,512]{1,0:T(1,128)} %bitcast.3, f32[1,8192]{1,0:T(1,128)} %bitcast.2, bf16[512,1024]{1,0:T(8,128)(2,1)} %k_hbm.1, bf16[512,1024]{1,0:T(8,128)(2,1)} %v_hbm.1, bf16[896,8192]{1,0:T(8,128)(2,1)} %wg_hbm.1, ...), custom_call_target="tpu_custom_call" | custom-call | tf_op jit(solution)/shard_map/pallas_call | solution.py:352
  56.2 1.4 %copy.11 = bf16[2,8192]{1,0:T(2,128)(2,1)} copy(bf16[2,8192]{1,0:T(2,128)(2,1)} %shard_map.91) | data formatting | bytes 65536

commit v3 on v2

--- a/solution.py
+++ b/solution.py
@@ -21,7 +21,7 @@
     k_v, v_v, wg, wu, wd, gathq, gathx, part, stats, square, gate_sum, up_sum, act, turn,
     pair_send, pair_recv, pst_send, pst_recv, chip_send, chip_recv, cst_send, cst_recv,
     pair2_send, pair2_recv, chip2_send, chip2_recv,
-    load_sem, w_sem, ag_send, ag_fwd, ag_recv, pr_send, pr_recv, ch_send, ch_recv,
+    load_sem, w_sem, ag_send, ag_fwd, ag_side, ag_recv, pr_send, pr_recv, ch_send, ch_recv,
 ):
     me = lax.axis_index("ctx")
     half = n // 2
@@ -81,33 +81,43 @@
         buf = (gathq, gathx)[which]
         return remote(buf.at[source], buf.at[source], send, ag_recv.at[which, source], to)
 
-    def source_of(k):
-        return lax.rem(chip + half - k, half)
+    twos = half // 2
+    two, side = chip // 2, lax.rem(chip, 2)
+    beside = 2 * (chip + 1 - 2 * side) + core
+
+    def source_of(i):
+        other = lax.rem(i, 2)
+        return 2 * lax.rem(two + twos - i // 2, twos) + side + other * (1 - 2 * side)
 
     def gather_start(which):
         def send(k):
-            to = 2 * lax.rem(chip + k, half) + core
+            to = 2 * (2 * lax.rem(two + k, twos) + side) + core
             gather_copy(which, me, to, ag_send.at[which, k]).start()
 
+        loop(1, twos, send)
+        gather_copy(which, me, beside, ag_send.at[which, twos]).start()
         gather_copy(which, me, partner, ag_send.at[which, 0]).start()
-        loop(1, half, send)
-
-    def forward(which, k):
-        source = 2 * source_of(k) + core
-        gather_copy(which, source, partner, ag_fwd.at[which, k]).wait_recv()
-        gather_copy(which, source, partner, ag_fwd.at[which, k]).start()
+
+    def forward(which, i):
+        source = 2 * source_of(i) + core
+        gather_copy(which, source, partner, ag_fwd.at[which, i]).wait_recv()
+
+        @pl.when(lax.rem(i, 2) == 0)
+        def _():
+            gather_copy(which, source, beside, ag_side.at[which, i // 2]).start()
+
+        gather_copy(which, source, partner, ag_fwd.at[which, i]).start()
 
     def arrive(which, p):
         gather_copy(which, 2 * p + 1 - core, partner, ag_send.at[which, 0]).wait_recv()
 
     def gather_end(which):
-        loop(0, half, lambda k: gather_copy(which, me, partner, ag_send.at[which, k]).wait_send())
-
-        def forwarded(k):
-            source = 2 * source_of(k) + core
-            gather_copy(which, source, partner, ag_fwd.at[which, k]).wait_send()
-
-        loop(1, half, forwarded)
+        def sent(sems):
+            return lambda k: gather_copy(which, me, partner, sems.at[which, k]).wait_send()
+
+        loop(0, twos + 1, sent(ag_send))
+        loop(1, half, sent(ag_fwd))
+        loop(1, twos, sent(ag_side))
 
     gather_start(0)
     for copy in w_copies:
@@ -137,11 +147,21 @@
     v_copy.wait()
 
     def pair_copy(which, p):
-        src, dst = ((pair_send, pair_recv), (pst_send, pst_recv), (pair2_send, pair2_recv))[which]
+        if which >= 2:
+            part_of = pl.ds((which - 2) * KEY_VALUE_HEADS // 2, KEY_VALUE_HEADS // 2)
+            src, dst = pair2_send.at[p, part_of], pair2_recv.at[p, part_of]
+            return remote(src, dst, pr_send.at[which, p], pr_recv.at[which, p], partner)
+        src, dst = ((pair_send, pair_recv), (pst_send, pst_recv))[which]
         return remote(src.at[p], dst.at[p], pr_send.at[which, p], pr_recv.at[which, p], partner)
 
     def chip_copy(which, p, slot):
-        src, dst = ((chip_send, chip_recv), (cst_send, cst_recv), (chip2_send, chip2_recv))[which]
+        if which >= 2:
+            part_of = pl.ds((which - 2) * KEY_VALUE_HEADS // 2, KEY_VALUE_HEADS // 2)
+            src, dst = chip2_send.at[p, part_of], chip2_recv.at[slot, part_of]
+            return remote(
+                src, dst, ch_send.at[which, p], ch_recv.at[which, slot], 2 * p + core
+            )
+        src, dst = ((chip_send, chip_recv), (cst_send, cst_recv))[which]
         return remote(
             src.at[p], dst.at[slot], ch_send.at[which, p], ch_recv.at[which, slot], 2 * p + core
         )
@@ -265,13 +285,14 @@
             first += size
 
     forward(1, 1)
+    forward(1, 2)
     arrive(1, chip)
     products(chip)
 
     def next_chip(k):
-        @pl.when(k + 1 < half)
+        @pl.when(k + 2 < half)
         def _():
-            forward(1, k + 1)
+            forward(1, k + 2)
 
         arrive(1, source_of(k))
         products(source_of(k))
@@ -294,33 +315,51 @@
         for h in range(GROUP):
             part[g, pl.ds(h, n * rows, stride=GROUP), :] = o[:, h * HEAD_SIZE : (h + 1) * HEAD_SIZE]
 
-    loop(0, KEY_VALUE_HEADS, down)
-
-    def to_pair2(j):
-        p = lax.rem(chip + 1 + j, half)
-        pair2_send[p] = part[:, slab(2 * p + 1 - core), :].astype(bf16)
-        pair_copy(2, p).start()
-
-    loop(0, half, to_pair2)
-
-    def merge2(p):
-        pair_copy(2, p).wait_recv()
-        return part[:, slab(2 * p + core), :] + pair2_recv[p].astype(f32)
-
-    def to_owner2(j):
-        p = lax.rem(chip + 1 + j, half)
-        chip2_send[p] = merge2(p).astype(bf16)
-        chip_copy(2, p, chip).start()
-
-    loop(0, half - 1, to_owner2)
-    mine = merge2(chip)
-
-    def add2(k, acc):
-        p = lax.rem(chip + half - k, half)
-        chip_copy(2, p, p).wait_recv()
-        return acc + chip2_recv[p].astype(f32)
-
-    turn[...] = lax.fori_loop(1, half, add2, mine)
+    middle = KEY_VALUE_HEADS // 2
+
+    def to_pair2(i):
+        heads = pl.ds(i * middle, middle)
+
+        def body(j):
+            p = lax.rem(chip + 1 + j, half)
+            pair2_send[p, heads] = part[heads, slab(2 * p + 1 - core), :].astype(bf16)
+            pair_copy(2 + i, p).start()
+
+        loop(0, half, body)
+
+    def merge2(i, p):
+        heads = pl.ds(i * middle, middle)
+        pair_copy(2 + i, p).wait_recv()
+        return part[heads, slab(2 * p + core), :] + pair2_recv[p, heads].astype(f32)
+
+    def to_owner2(i):
+        def body(j):
+            p = lax.rem(chip + 1 + j, half)
+            chip2_send[p, pl.ds(i * middle, middle)] = merge2(i, p).astype(bf16)
+            chip_copy(2 + i, p, chip).start()
+
+        loop(0, half - 1, body)
+        turn[pl.ds(i * middle, middle)] = merge2(i, chip)
+
+    def add2(i):
+        heads = pl.ds(i * middle, middle)
+
+        def body(k, acc):
+            p = source_of(k)
+            chip_copy(2 + i, p, p).wait_recv()
+            return acc + chip2_recv[p, heads].astype(f32)
+
+        turn[heads] = lax.fori_loop(1, half, body, turn[heads])
+
+    loop(0, middle, down)
+    to_pair2(0)
+    loop(middle, middle + 2, down)
+    to_owner2(0)
+    loop(middle + 2, KEY_VALUE_HEADS, down)
+    to_pair2(1)
+    to_owner2(1)
+    add2(0)
+    add2(1)
     out_ref[...] = jnp.concatenate(
         [
             turn[g, pl.ds(h, rows, stride=GROUP), :]
@@ -330,6 +369,7 @@
         axis=1,
     ).astype(bf16)
     finish_sends(2)
+    finish_sends(3)
 
 
 def local(queries, keys, values, position, lengths, gain, gate_weight, up_weight, down_weight):
@@ -373,8 +413,8 @@
             heads(), heads(), state(), state(),
             data(), data(), data(), data(),
             dma((2,)), dma((3, PIECES)),
-            dma((2, half)), dma((2, half)), dma((2, n)),
-            dma((3, half)), dma((3, half)), dma((3, half)), dma((3, half)),
+            dma((2, half // 2 + 1)), dma((2, half)), dma((2, half // 2)), dma((2, n)),
+            dma((4, half)), dma((4, half)), dma((4, half)), dma((4, half)),
         ],
         compiler_params=pltpu.CompilerParams(
             collective_id=0, has_side_effects=True, vmem_limit_bytes=60 * 2**20

time: 57.9 us -> 64.6 us (1.12)
  Pallas kernels: 56.2 us -> 63 us
    pallas_call x1, Pallas kernels: 56.2 us -> 63 us  [local(): pl.pallas_call(functools.partial(kernel, n, rows), out_shape=jax.ShapeDty...]
where the time goes in v3:
time: 64.6 us; the launch traced here: 64.4 us
  Pallas kernels  63 us (98%)
  local copies, waits for them, and re-layouts  1.4 us (2%)
    pallas_call x1, Pallas kernels, local(): pl.pallas_call(functools.partial(kernel, n, rows), out_shape=jax.ShapeDty...  63 us
    unnamed x1, local copies, waits for them, and re-layouts  1.4 us

profile of v3, /device:TPU:0, one launch (start us, length us, event | category | flops | bytes accessed | tf_op | source)
XLA Modules:
  0.0 64.4 jit_solution(18372631276812786287)
XLA Ops:
  0.0 63.0 %shard_map.91 = bf16[2,8192]{1,0:T(2,128)(2,1)} custom-call(s32[2]{0:T(128)} %len_ref.1, bf16[2,8192]{1,0:T(2,128)(2,1)} %q_ref.1, s32[1,512]{1,0:T(1,128)} %bitcast.3, f32[1,8192]{1,0:T(1,128)} %bitcast.2, bf16[512,1024]{1,0:T(8,128)(2,1)} %k_hbm.1, bf16[512,1024]{1,0:T(8,128)(2,1)} %v_hbm.1, bf16[896,8192]{1,0:T(8,128)(2,1)} %wg_hbm.1, ...), custom_call_target="tpu_custom_call" | custom-call | tf_op jit(solution)/shard_map/pallas_call | solution.py:392
  63.0 1.4 %copy.11 = bf16[2,8192]{1,0:T(2,128)(2,1)} copy(bf16[2,8192]{1,0:T(2,128)(2,1)} %shard_map.91) | data formatting | bytes 65536
